TPU v7x, 32 devices: a whole 2x2x4 slice. The times are simulated.
32 devices in a mesh: cfg: 2 (over x), space: 16 (over z, y, core).
Axes of the slice: x: 2, y: 2, z: 4, core: 2. Of those that a mesh axis runs over, the one named last changes fastest.
Arguments:
- vectors: float32 [4, 2, 3, 2048, 256], P('cfg', None, None, 'space'), parts along dimension 0, may hold values from -1.75 to 1.75
- links: float32 [4, 3, 2, 3, 3, 2048], P('cfg', None, None, None, None, 'space'), parts along dimension 0, may hold values from -2.5 to 2.5
- directions: int32 [3], replicated, may hold values from 0 to 2
- slice_group: int32 [2], replicated, may hold values from 0 to 1, as said below
- peram: float32 [4, 1024, 1024], P('cfg', None, 'space'), parts along dimension 0, may hold values from -0.3125 to 0.3125
- block_group: int32 [16], P('space'), may hold values from 0 to 1
Outputs:
- elementals: float32 [4, 3, 2, 256, 256], P('cfg', None, None, 'space'), parts along dimension 0
- blocks: float32 [4, 1024, 64], P('cfg', 'space'), parts along dimension 0
There are 2 independent parts, one for each index of `cfg`. A program takes and returns all parts, laid end to end along the dimension named above; an argument that names none is the same for every part. Nothing has to cross between parts.
Inputs may be any that keep to these rules, and one draw needn't show every extreme that they name: `slice_group`: every group holds at least one timeslice.
All inputs are finite; a program needn't handle non-finite values.
Results may differ from a plain program's by a relative error of at most 0.0001.
Values sent between devices are 32-bit elements; how exact they have to be, the bound alone decides.
A program may use at most 64 MiB of HBM per device.

v0:
```python
import functools

import jax
import jax.numpy as jnp
from jax import lax
from jax.experimental import pallas as pl
from jax.experimental.pallas import tpu as pltpu
from jax.sharding import PartitionSpec as P

NG = 2
LZ = 16
MESH = pl.DeviceIdType.MESH
precise = lax.Precision.HIGHEST
f32 = jnp.float32
bf16 = jnp.bfloat16


def split(value):
    high = value.astype(bf16)
    return high, (value - high.astype(f32)).astype(bf16)


def kernel(
    n, vec, lnk, per, dirs, sgroup, bgroup, elem, blocks,
    pvec, zvec, edge, plnk, zlnk, ut, lth, ltl, xh, xl, acc, part, recv, full, tcol,
    rhsh, rhsl, send_sem, recv_sem,
):
    sites = vec.shape[3]
    nv = vec.shape[4]
    cb = per.shape[2]
    rl = nv // n
    me = lax.axis_index("space")
    cfg = lax.axis_index("cfg")
    core = lax.rem(me, 2)
    b = lax.rem(me // 2, 2)

    def flip(mask):
        return me + mask * (1 - 2 * lax.rem(me // mask, 2))

    up = lax.rem(me + 4, n)
    down = lax.rem(me + n - 4, n)
    zmasks = []
    mask = 4
    while mask < n:
        zmasks.append(mask)
        mask *= 2
    others = [flip(1), flip(2), up, down] + [flip(m) for m in zmasks]
    barrier = pltpu.get_barrier_semaphore()
    for other in others:
        pl.semaphore_signal(barrier, inc=1, device_id=(cfg, other), device_id_type=MESH)
    pl.semaphore_wait(barrier, len(others))

    used = [0]

    def send(src, dst, other):
        i = used[0]
        used[0] += 1
        copy = pltpu.make_async_remote_copy(
            src_ref=src, dst_ref=dst, send_sem=send_sem.at[i], recv_sem=recv_sem.at[i],
            device_id=(cfg, other), device_id_type=MESH,
        )
        copy.start()
        return copy

    partner, mate = flip(2), flip(1)
    zdst = lax.rem(me + n + 8 * b - 4, n)
    got_edge = send(vec.at[b, :, :, pl.ds(0, LZ), :], edge.at[0], mate)
    got_plnk = send(lnk.at[1 - b], plnk, partner)
    got_zlnk = send(lnk.at[b], zlnk, zdst)
    got_pvec = send(vec.at[1 - b], pvec, partner)
    got_zvec = send(vec.at[b], zvec, zdst)

    def set_left(get):
        for ri in range(2):
            for c in range(3):
                j = ri * 3 + c
                high, low = split(jnp.transpose(get(ri, c)))
                lth[:, j * sites:(j + 1) * sites] = high
                ltl[:, j * sites:(j + 1) * sites] = low

    step = 16

    def derive(slot, column, fetch):
        def chunk(q, carry):
            base = pl.multiple_of(q * step, step)
            rows = pl.ds(base, step)
            link = ut[slot, rows, :]
            out_r = [None] * 3
            out_i = [None] * 3
            for c in range(3):
                vr = fetch(0, c, q, base)
                vi = fetch(1, c, q, base)
                for r in range(3):
                    j = column + r * 3 + c
                    lr = jnp.broadcast_to(link[:, j:j + 1], (step, nv))
                    li = jnp.broadcast_to(link[:, j + 9:j + 10], (step, nv))
                    tr = lr * vr - li * vi
                    ti = lr * vi + li * vr
                    out_r[r] = tr if c == 0 else out_r[r] + tr
                    out_i[r] = ti if c == 0 else out_i[r] + ti
            for r in range(3):
                plus = out_r[r] + out_i[r]
                minus = out_i[r] - out_r[r]
                ph, plo = split(plus)
                mh, mlo = split(minus)
                first = pl.ds(pl.multiple_of(r * sites + base, step), step)
                second = pl.ds(pl.multiple_of((3 + r) * sites + base, step), step)
                xh[first, :nv] = ph
                xl[first, :nv] = plo
                xh[second, :nv] = mh
                xl[second, :nv] = mlo
                xh[first, nv:] = mh
                xl[first, nv:] = mlo
                xh[second, nv:] = -ph
                xl[second, nv:] = -plo
            return carry

        lax.fori_loop(0, sites // step, chunk, 0)

    def contract(direction, first):
        prod = jnp.dot(lth[...], xh[...], preferred_element_type=f32)
        prod += jnp.dot(lth[...], xl[...], preferred_element_type=f32)
        prod += jnp.dot(ltl[...], xh[...], preferred_element_type=f32)
        if first:
            acc[direction] = prod
        else:
            acc[direction] += prod

    def set_links(slot, rows):
        ut[slot] = jnp.transpose(rows)

    def fetch_plain(get):
        return lambda ri, c, q, base: get(ri, c, pl.ds(base, step))

    def fetch_z(get):
        def fetch(ri, c, q, base):
            block = get(ri, c, pl.ds(base, step))
            return jnp.concatenate([block[1:], block[:1]], axis=0)
        return fetch

    def fetch_y(get, k):
        count = sites // LZ

        def fetch(ri, c, q, base):
            start = pl.multiple_of(lax.rem(q + 1, count) * step, step)
            inner = get(ri, c, pl.ds(start, step))
            return jnp.where(q == count - 1, edge[k, ri, c], inner)
        return fetch

    def own(ri, c, rows):
        return vec[b, ri, c, rows, :]

    def theirs(ri, c, rows):
        return pvec[ri, c, rows, :]

    def beyond(ri, c, rows):
        return zvec[ri, c, rows, :]

    everything = pl.ds(0, sites)
    set_left(lambda ri, c: own(ri, c, everything))
    set_links(0, lnk[b])
    derive(0, 36, fetch_z(own))
    contract(2, True)
    got_edge.wait()
    derive(0, 18, fetch_y(own, 0))
    contract(1, True)

    lo = [[per[ri, (2 + s) * nv:(3 + s) * nv, :] for ri in range(2)] for s in range(2)]
    turned = [
        [lo[1], lo[0]],
        [[lo[1][1], -lo[1][0]], [-lo[0][1], lo[0][0]]],
        [lo[0], [-lo[1][0], -lo[1][1]]],
    ]
    for k in range(3):
        (ar, ai), (br, bi) = turned[k]
        high, low = split(jnp.concatenate([ar, br, ai, bi], axis=1))
        rhsh[2 * k * nv:(2 * k + 1) * nv, :] = high
        rhsl[2 * k * nv:(2 * k + 1) * nv, :] = low
        high, low = split(jnp.concatenate([-ai, -bi, ar, br], axis=1))
        rhsh[(2 * k + 1) * nv:(2 * k + 2) * nv, :] = high
        rhsl[(2 * k + 1) * nv:(2 * k + 2) * nv, :] = low

    got_plnk.wait()
    got_zlnk.wait()
    set_links(1, plnk[...])

    def turn(ahead, behind):
        rows = []
        for ri in range(2):
            for r in range(3):
                for c in range(3):
                    j, k = ri * 9 + r * 3 + c, ri * 9 + c * 3 + r
                    back = -behind[k:k + 1] if ri == 0 else behind[k:k + 1]
                    rows.append(jnp.where(b == 0, ahead[j:j + 1], back))
        rows.append(jnp.zeros((64 - 18, sites), f32))
        return jnp.concatenate(rows, axis=0)

    set_links(2, turn(lnk[b, 0:18], plnk[0:18]))
    set_links(3, turn(plnk[0:18], zlnk[0:18]))

    got_pvec.wait()
    got_pedge = send(pvec.at[:, :, pl.ds(0, LZ), :], edge.at[1], mate)
    derive(2, 0, fetch_plain(theirs))
    contract(0, True)
    set_left(lambda ri, c: theirs(ri, c, everything))
    derive(1, 36, fetch_z(theirs))
    contract(2, False)
    got_pedge.wait()
    derive(1, 18, fetch_y(theirs, 1))
    contract(1, False)
    got_zvec.wait()
    derive(3, 0, fetch_plain(beyond))
    contract(0, False)
    for k in range(3):
        part[k * nv:(k + 1) * nv, :] = acc[k, :, :nv] + jnp.transpose(acc[k, :, nv:])

    offset = 0
    size = 3 * nv
    place = 0
    trail = []
    for m in [1] + zmasks:
        size //= 2
        bit = lax.rem(me // m, 2)
        kept = pl.multiple_of(offset + bit * size, 8)
        sent = pl.multiple_of(offset + (1 - bit) * size, 8)
        landing = pl.ds(place, size)
        copy = send(part.at[pl.ds(sent, size), :], recv.at[landing, :], flip(m))
        copy.wait()
        trail.append((m, kept, size))
        if m == ([1] + zmasks)[-1]:
            full[b, pl.ds(kept, size), :] = part[pl.ds(kept, size), :] + recv[landing, :]
        else:
            part[pl.ds(kept, size), :] += recv[landing, :]
        offset = kept
        place += size

    def share(t, at, rows, other):
        where = full.at[t, pl.ds(at, rows), :]
        return send(where, where, other)

    for m, kept, size in reversed(trail[1:]):
        share(b, kept, size, flip(m)).wait()
    _, kept, size = trail[0]
    over_y = share(b, kept, size, partner)
    over_core = share(b, kept, size, mate)
    over_core.wait()

    column = me * rl
    lane = pl.multiple_of((column // 128) * 128, 128)
    inside = column - lane

    def columns_of(t):
        for i in range(3):
            tcol[t, i] = jnp.transpose(full[t, i * nv:(i + 1) * nv, pl.ds(lane, 128)])

    columns_of(b)
    over_y.wait()
    share(1 - b, kept, size, mate).wait()
    columns_of(1 - b)

    def hot(condition):
        return jnp.where(condition, 1.0, 0.0).astype(f32)

    in_dir = [[hot(dirs[k] == i) for i in range(3)] for k in range(3)]
    in_group = [[hot(sgroup[t] == g) for t in range(2)] for g in range(NG)]
    my_group = [hot(bgroup[0] == g) for g in range(NG)]
    in_block = [sum(my_group[g] * in_group[g][t] for g in range(NG)) for t in range(2)]

    def rows_at(get, start):
        if rl % 8 == 0:
            return get(pl.ds(pl.multiple_of(start, 8), rl))
        base = pl.multiple_of((start // 8) * 8, 8)
        block = get(pl.ds(base, 8))
        rows = block[:rl]
        for j in range(1, 8 // rl):
            rows = jnp.where(start - base == j * rl, block[j * rl:(j + 1) * rl], rows)
        return rows

    plain = [
        [rows_at(lambda at: full[t, at, :], i * nv + column) for i in range(3)] for t in range(2)
    ]
    flipped = [[rows_at(lambda at: tcol[t, i, at, :], inside) for i in range(3)] for t in range(2)]
    for k in range(3):
        fwd = [sum(in_dir[k][i] * plain[t][i] for i in range(3)) for t in range(2)]
        bwd = [sum(in_dir[k][i] * flipped[t][i] for i in range(3)) for t in range(2)]
        for g in range(NG):
            one = in_group[g][0] * fwd[0] + in_group[g][1] * fwd[1]
            two = in_group[g][0] * bwd[0] + in_group[g][1] * bwd[1]
            elem[g, k, 0] = 0.25 * (one - two)
            elem[g, k, 1] = 0.25 * (one + two)

    total = jnp.zeros((nv, 4 * cb), f32)
    for k in range(3):
        chosen = jnp.zeros((nv, nv), f32)
        for t in range(2):
            for i in range(3):
                chosen += (in_block[t] * in_dir[k][i]) * full[t, i * nv:(i + 1) * nv, :]
        other = jnp.transpose(chosen)
        for ri, mat in enumerate((0.25 * (chosen - other), 0.25 * (chosen + other))):
            high, low = split(mat)
            rows = slice((2 * k + ri) * nv, (2 * k + ri + 1) * nv)
            total += jnp.dot(high, rhsh[rows, :], preferred_element_type=f32)
            total += jnp.dot(high, rhsl[rows, :], preferred_element_type=f32)
            total += jnp.dot(low, rhsh[rows, :], preferred_element_type=f32)

    zr = jnp.zeros((cb, cb), f32)
    zi = jnp.zeros((cb, cb), f32)
    for a in range(2):
        ur = jnp.transpose(per[0, a * nv:(a + 1) * nv, :])
        ui = jnp.transpose(per[1, a * nv:(a + 1) * nv, :])
        yr = total[:, a * cb:(a + 1) * cb]
        yi = total[:, (2 + a) * cb:(3 + a) * cb]
        dot = functools.partial(jnp.dot, precision=precise, preferred_element_type=f32)
        zr += dot(ur, yr) + dot(ui, yi)
        zi += dot(ur, yi) - dot(ui, yr)
    blocks[0] = zi - jnp.transpose(zi)
    blocks[1] = -(zr + jnp.transpose(zr))


def body(vectors, links, directions, slice_group, peram, block_group, *, n):
    nt, _, _, sites, nv = vectors.shape
    cb = peram.shape[2]
    lnk = jnp.pad(links.reshape(nt, 54, sites), ((0, 0), (0, 10), (0, 0)))
    vmem = pl.BlockSpec(memory_space=pltpu.VMEM)
    smem = pl.BlockSpec(memory_space=pltpu.SMEM)
    copies = 32
    return pl.pallas_call(
        functools.partial(kernel, n),
        out_shape=(
            jax.ShapeDtypeStruct((NG, 3, 2, nv // n, nv), f32),
            jax.ShapeDtypeStruct((2, cb, cb), f32),
        ),
        in_specs=[vmem, vmem, vmem, smem, smem, smem],
        out_specs=(vmem, vmem),
        scratch_shapes=[
            pltpu.VMEM((2, 3, sites, nv), f32),
            pltpu.VMEM((2, 3, sites, nv), f32),
            pltpu.VMEM((2, 2, 3, LZ, nv), f32),
            pltpu.VMEM((64, sites), f32),
            pltpu.VMEM((64, sites), f32),
            pltpu.VMEM((4, sites, 64), f32),
            pltpu.VMEM((nv, 6 * sites), bf16),
            pltpu.VMEM((nv, 6 * sites), bf16),
            pltpu.VMEM((6 * sites, 2 * nv), bf16),
            pltpu.VMEM((6 * sites, 2 * nv), bf16),
            pltpu.VMEM((3, nv, 2 * nv), f32),
            pltpu.VMEM((3 * nv, nv), f32),
            pltpu.VMEM((3 * nv, nv), f32),
            pltpu.VMEM((2, 3 * nv, nv), f32),
            pltpu.VMEM((2, 3, 128, nv), f32),
            pltpu.VMEM((6 * nv, 4 * cb), bf16),
            pltpu.VMEM((6 * nv, 4 * cb), bf16),
            pltpu.SemaphoreType.DMA((copies,)),
            pltpu.SemaphoreType.DMA((copies,)),
        ],
        compiler_params=pltpu.CompilerParams(
            collective_id=0, has_side_effects=True, vmem_limit_bytes=48 * 2**20
        ),
    )(vectors, lnk, peram, directions, slice_group, block_group)


def solution(mesh):
    return jax.shard_map(
        functools.partial(body, n=mesh.shape["space"]),
        mesh=mesh,
        in_specs=(
            P("cfg", None, None, "space", None),
            P("cfg", None, None, None, None, "space"),
            P(),
            P(),
            P("cfg", None, "space"),
            P("space"),
        ),
        out_specs=(P("cfg", None, None, "space", None), P("cfg", "space", None)),
        check_vma=False,
    )
```

profile of v0, /device:TPU:0, one launch (start us, length us, event | category | flops | bytes accessed | tf_op | source)
XLA Modules:
  0.0 74.8 jit_solution(8041655715705857162)
XLA Ops:
  0.6 0.0 copy-start.2
  0.6 0.0 copy-start.1
  0.7 0.0 copy-start
  1.4 0.8 %copy.10 = f32[2,3,2,3,3,128]{5,0,4,3,2,1:T(2,128)S(1)} copy(f32[2,3,2,3,3,128]{5,2,4,3,1,0:T(2,128)} %param.7) | data formatting | bytes 110592 | tf_op args[1]
  2.3 1.4 %copy.12.per = f32[2,1024,64]{2,1,0:T(8,128)S(1)} copy(f32[2,1024,64]{1,2,0:T(8,128)} %param.10) | data formatting | bytes 1048576 | tf_op args[4]
  3.7 0.0 copy-done.2
  3.7 0.0 copy-done.1
  3.7 0.0 copy-done
  3.7 69.7 %shard_map.77 = (f32[2,3,2,16,256]{4,3,2,1,0:T(8,128)S(1)}, f32[2,64,64]{2,1,0:T(8,128)S(1)}) custom-call(f32[2,2,3,128,256]{4,3,2,1,0:T(8,128)S(1)} %copy-done, f32[2,64,128]{2,1,0:T(8,128)S(1)} %pad.4.lnk, f32[2,1024,64]{2,1,0:T(8,128)S(1)} %copy.12.per, s32[3]{0:T(128)S(1)} %copy-done.1, s32[2]{0:T(128)S(1)} %copy-done.2, s32[1]{0:T(128)S(6)} %copy.15.bgroup), custom_call_target="tpu_custom_call" | custom-call | tf_op jit(solution)/shard_map/pallas_call | solution.py:327
  73.5 0.7 copy.16
  74.1 0.6 copy.17
  (2 shorter events, 0.0 us)
Async XLA Ops:
  0.6 3.1 %copy-start.2 = (s32[2]{0:T(128)S(1)}, s32[2]{0:T(128)}, u32[]{:S(2)}) copy-start(s32[2]{0:T(128)} %sgroup.1) | copy-start | bytes 28
  0.6 3.1 %copy-start.1 = (s32[3]{0:T(128)S(1)}, s32[3]{0:T(128)}, u32[]{:S(2)}) copy-start(s32[3]{0:T(128)} %dirs.1) | copy-start | bytes 40
  0.7 3.1 %copy-start = (f32[2,2,3,128,256]{4,3,2,1,0:T(8,128)S(1)}, f32[2,2,3,128,256]{4,3,2,1,0:T(8,128)}, u32[]{:S(2)}) copy-start(f32[2,2,3,128,256]{4,3,2,1,0:T(8,128)} %vec.1) | copy-start | bytes 4718596
where the time goes:
time: 75 us; the launch traced here: 74.8 us
  Pallas kernels  69.7 us (93%)
  local copies, waits for them, and re-layouts  3.55 us (5%)
  between operations  1.48 us (2%)
    pallas_call x1, Pallas kernels, body(): pl.pallas_call(functools.partial(kernel, n), out_shape=(jax.ShapeDtypeStr...  69.7 us
    unnamed x10, local copies, waits for them, and re-layouts  3.54 us

commit v1 on v0

--- a/solution.py
+++ b/solution.py
@@ -10,7 +10,6 @@
 NG = 2
 LZ = 16
 MESH = pl.DeviceIdType.MESH
-precise = lax.Precision.HIGHEST
 f32 = jnp.float32
 bf16 = jnp.bfloat16
 
@@ -23,11 +22,11 @@
 def kernel(
     n, vec, lnk, per, dirs, sgroup, bgroup, elem, blocks,
     pvec, zvec, edge, plnk, zlnk, ut, lth, ltl, xh, xl, acc, part, recv, full, tcol,
-    rhsh, rhsl, send_sem, recv_sem,
+    perh, perl, pper, rows_out, rows_in, res_own, res_out, res_in, send_sem, recv_sem,
 ):
     sites = vec.shape[3]
     nv = vec.shape[4]
-    cb = per.shape[2]
+    cb = per.shape[1]
     rl = nv // n
     me = lax.axis_index("space")
     cfg = lax.axis_index("cfg")
@@ -165,20 +164,23 @@
     derive(0, 18, fetch_y(own, 0))
     contract(1, True)
 
-    lo = [[per[ri, (2 + s) * nv:(3 + s) * nv, :] for ri in range(2)] for s in range(2)]
-    turned = [
-        [lo[1], lo[0]],
-        [[lo[1][1], -lo[1][0]], [-lo[0][1], lo[0][0]]],
-        [lo[0], [-lo[1][0], -lo[1][1]]],
-    ]
-    for k in range(3):
-        (ar, ai), (br, bi) = turned[k]
-        high, low = split(jnp.concatenate([ar, br, ai, bi], axis=1))
-        rhsh[2 * k * nv:(2 * k + 1) * nv, :] = high
-        rhsl[2 * k * nv:(2 * k + 1) * nv, :] = low
-        high, low = split(jnp.concatenate([-ai, -bi, ar, br], axis=1))
-        rhsh[(2 * k + 1) * nv:(2 * k + 2) * nv, :] = high
-        rhsl[(2 * k + 1) * nv:(2 * k + 2) * nv, :] = low
+    def set_peram(slot, source):
+        lo = [[source[ri, :, (2 + s) * nv:(3 + s) * nv] for ri in range(2)] for s in range(2)]
+        turned = [
+            [lo[1], lo[0]],
+            [[lo[1][1], -lo[1][0]], [-lo[0][1], lo[0][0]]],
+            [lo[0], [-lo[1][0], -lo[1][1]]],
+        ]
+        rows = slice(slot * 4 * cb, (slot + 1) * 4 * cb)
+        for k in range(3):
+            (ar, ai), (br, bi) = turned[k]
+            for part_of, stacked in enumerate(([ar, br, ai, bi], [-ai, -bi, ar, br])):
+                high, low = split(jnp.concatenate(stacked, axis=0))
+                lanes = slice((2 * k + part_of) * nv, (2 * k + part_of + 1) * nv)
+                perh[rows, lanes] = high
+                perl[rows, lanes] = low
+
+    set_peram(0, per)
 
     got_plnk.wait()
     got_zlnk.wait()
@@ -198,65 +200,72 @@
     set_links(2, turn(lnk[b, 0:18], plnk[0:18]))
     set_links(3, turn(plnk[0:18], zlnk[0:18]))
 
+    stages = [1] + zmasks
+
+    def reduce_and_share(i):
+        offset = 0
+        size = nv
+        place = 0
+        trail = []
+        for m in stages:
+            size //= 2
+            bit = lax.rem(me // m, 2)
+            kept = pl.multiple_of(offset + bit * size, 8)
+            sent = pl.multiple_of(offset + (1 - bit) * size, 8)
+            landing = pl.ds(place, size)
+            copy = send(part.at[i, pl.ds(sent, size), :], recv.at[i, landing, :], flip(m))
+            yield
+            copy.wait()
+            trail.append((m, kept, size))
+            total = part[i, pl.ds(kept, size), :] + recv[i, landing, :]
+            if m == stages[-1]:
+                full[i, pl.ds(kept, size), :] = total
+            else:
+                part[i, pl.ds(kept, size), :] = total
+            offset = kept
+            place += size
+        for m, kept, size in reversed(trail):
+            where = full.at[i, pl.ds(kept, size), :]
+            copy = send(where, where, flip(m))
+            yield
+            copy.wait()
+
+    def finish(k):
+        part[k] = acc[k, :, :nv] + jnp.transpose(acc[k, :, nv:])
+
     got_pvec.wait()
     got_pedge = send(pvec.at[:, :, pl.ds(0, LZ), :], edge.at[1], mate)
+    got_pper = send(per, pper, partner)
     derive(2, 0, fetch_plain(theirs))
     contract(0, True)
     set_left(lambda ri, c: theirs(ri, c, everything))
     derive(1, 36, fetch_z(theirs))
     contract(2, False)
+    finish(2)
+    moving_z = reduce_and_share(2)
+    next(moving_z)
     got_pedge.wait()
     derive(1, 18, fetch_y(theirs, 1))
+    next(moving_z)
     contract(1, False)
+    finish(1)
+    moving_y = reduce_and_share(1)
+    next(moving_y)
     got_zvec.wait()
     derive(3, 0, fetch_plain(beyond))
+    next(moving_z)
+    next(moving_y)
     contract(0, False)
-    for k in range(3):
-        part[k * nv:(k + 1) * nv, :] = acc[k, :, :nv] + jnp.transpose(acc[k, :, nv:])
-
-    offset = 0
-    size = 3 * nv
-    place = 0
-    trail = []
-    for m in [1] + zmasks:
-        size //= 2
-        bit = lax.rem(me // m, 2)
-        kept = pl.multiple_of(offset + bit * size, 8)
-        sent = pl.multiple_of(offset + (1 - bit) * size, 8)
-        landing = pl.ds(place, size)
-        copy = send(part.at[pl.ds(sent, size), :], recv.at[landing, :], flip(m))
-        copy.wait()
-        trail.append((m, kept, size))
-        if m == ([1] + zmasks)[-1]:
-            full[b, pl.ds(kept, size), :] = part[pl.ds(kept, size), :] + recv[landing, :]
-        else:
-            part[pl.ds(kept, size), :] += recv[landing, :]
-        offset = kept
-        place += size
-
-    def share(t, at, rows, other):
-        where = full.at[t, pl.ds(at, rows), :]
-        return send(where, where, other)
-
-    for m, kept, size in reversed(trail[1:]):
-        share(b, kept, size, flip(m)).wait()
-    _, kept, size = trail[0]
-    over_y = share(b, kept, size, partner)
-    over_core = share(b, kept, size, mate)
-    over_core.wait()
-
-    column = me * rl
-    lane = pl.multiple_of((column // 128) * 128, 128)
-    inside = column - lane
-
-    def columns_of(t):
-        for i in range(3):
-            tcol[t, i] = jnp.transpose(full[t, i * nv:(i + 1) * nv, pl.ds(lane, 128)])
-
-    columns_of(b)
-    over_y.wait()
-    share(1 - b, kept, size, mate).wait()
-    columns_of(1 - b)
+    finish(0)
+    moving_x = reduce_and_share(0)
+    moving = [moving_z, moving_y, moving_x]
+    first = True
+    while moving:
+        moving = [one for one in moving if next(one, 0) is None]
+        if first:
+            first = False
+            got_pper.wait()
+            set_peram(1, pper)
 
     def hot(condition):
         return jnp.where(condition, 1.0, 0.0).astype(f32)
@@ -265,6 +274,10 @@
     in_group = [[hot(sgroup[t] == g) for t in range(2)] for g in range(NG)]
     my_group = [hot(bgroup[0] == g) for g in range(NG)]
     in_block = [sum(my_group[g] * in_group[g][t] for g in range(NG)) for t in range(2)]
+
+    lane = pl.multiple_of(((me * rl) // 128) * 128, 128)
+    for i in range(3):
+        tcol[i] = jnp.transpose(full[i, :, pl.ds(lane, 128)])
 
     def rows_at(get, start):
         if rl % 8 == 0:
@@ -276,45 +289,63 @@
             rows = jnp.where(start - base == j * rl, block[j * rl:(j + 1) * rl], rows)
         return rows
 
-    plain = [
-        [rows_at(lambda at: full[t, at, :], i * nv + column) for i in range(3)] for t in range(2)
-    ]
-    flipped = [[rows_at(lambda at: tcol[t, i, at, :], inside) for i in range(3)] for t in range(2)]
+    def rows_of(device, i):
+        plain = rows_at(lambda at: full[i, at, :], device * rl)
+        flipped = rows_at(lambda at: tcol[i, at, :], device * rl - lane)
+        return 0.25 * (plain - flipped), 0.25 * (plain + flipped)
+
+    for i in range(3):
+        for ri, value in enumerate(rows_of(partner, i)):
+            rows_out[i, ri, :rl] = value
+    got_rows = send(rows_out, rows_in, partner)
+
+    total = jnp.zeros((8 * cb, nv), f32)
     for k in range(3):
-        fwd = [sum(in_dir[k][i] * plain[t][i] for i in range(3)) for t in range(2)]
-        bwd = [sum(in_dir[k][i] * flipped[t][i] for i in range(3)) for t in range(2)]
-        for g in range(NG):
-            one = in_group[g][0] * fwd[0] + in_group[g][1] * fwd[1]
-            two = in_group[g][0] * bwd[0] + in_group[g][1] * bwd[1]
-            elem[g, k, 0] = 0.25 * (one - two)
-            elem[g, k, 1] = 0.25 * (one + two)
-
-    total = jnp.zeros((nv, 4 * cb), f32)
+        chosen = sum(in_dir[k][i] * full[i] for i in range(3))
+        other = jnp.transpose(chosen)
+        for ri, mat in enumerate((0.25 * (other - chosen), 0.25 * (chosen + other))):
+            high, low = split(mat)
+            lanes = slice((2 * k + ri) * nv, (2 * k + ri + 1) * nv)
+            total += jnp.dot(perh[:, lanes], high, preferred_element_type=f32)
+            total += jnp.dot(perl[:, lanes], high, preferred_element_type=f32)
+            total += jnp.dot(perh[:, lanes], low, preferred_element_type=f32)
+
+    def against(left, right):
+        return lax.dot_general(
+            left, right, (((1,), (1,)), ((), ())), preferred_element_type=f32
+        )
+
+    def sided(slot, source, out):
+        mine = total[slot * 4 * cb:(slot + 1) * 4 * cb]
+        real = jnp.concatenate([mine[:cb], mine[cb:2 * cb]], axis=1)
+        imag = jnp.concatenate([mine[2 * cb:3 * cb], mine[3 * cb:]], axis=1)
+        yh, yl = split(jnp.concatenate([real, imag], axis=0))
+        uh, ul = split(
+            jnp.concatenate([source[0, :, :2 * nv], source[1, :, :2 * nv]], axis=0)
+        )
+        quads = against(uh, yh) + against(uh, yl) + against(ul, yh)
+        zr = quads[:cb, :cb] + quads[cb:, cb:]
+        zi = quads[:cb, cb:] - quads[cb:, :cb]
+        out[0] = zi - jnp.transpose(zi)
+        out[1] = -(zr + jnp.transpose(zr))
+
+    sided(1, pper, res_out)
+    got_res = send(res_out, res_in, partner)
+    sided(0, per, res_own)
+
+    mine = [rows_of(me, i) for i in range(3)]
+    got_rows.wait()
+    yours = [[rows_in[i, ri, :rl] for ri in range(2)] for i in range(3)]
     for k in range(3):
-        chosen = jnp.zeros((nv, nv), f32)
-        for t in range(2):
-            for i in range(3):
-                chosen += (in_block[t] * in_dir[k][i]) * full[t, i * nv:(i + 1) * nv, :]
-        other = jnp.transpose(chosen)
-        for ri, mat in enumerate((0.25 * (chosen - other), 0.25 * (chosen + other))):
-            high, low = split(mat)
-            rows = slice((2 * k + ri) * nv, (2 * k + ri + 1) * nv)
-            total += jnp.dot(high, rhsh[rows, :], preferred_element_type=f32)
-            total += jnp.dot(high, rhsl[rows, :], preferred_element_type=f32)
-            total += jnp.dot(low, rhsh[rows, :], preferred_element_type=f32)
-
-    zr = jnp.zeros((cb, cb), f32)
-    zi = jnp.zeros((cb, cb), f32)
-    for a in range(2):
-        ur = jnp.transpose(per[0, a * nv:(a + 1) * nv, :])
-        ui = jnp.transpose(per[1, a * nv:(a + 1) * nv, :])
-        yr = total[:, a * cb:(a + 1) * cb]
-        yi = total[:, (2 + a) * cb:(3 + a) * cb]
-        dot = functools.partial(jnp.dot, precision=precise, preferred_element_type=f32)
-        zr += dot(ur, yr) + dot(ui, yi)
-        zi += dot(ur, yi) - dot(ui, yr)
-    blocks[0] = zi - jnp.transpose(zi)
-    blocks[1] = -(zr + jnp.transpose(zr))
+        for ri in range(2):
+            here = sum(in_dir[k][i] * mine[i][ri] for i in range(3))
+            there = sum(in_dir[k][i] * yours[i][ri] for i in range(3))
+            by_time = [jnp.where(b == t, here, there) for t in range(2)]
+            for g in range(NG):
+                elem[g, k, ri] = in_group[g][0] * by_time[0] + in_group[g][1] * by_time[1]
+    got_res.wait()
+    weight = [jnp.where(b == 0, in_block[0], in_block[1]), jnp.where(b == 0, in_block[1], in_block[0])]
+    blocks[...] = weight[0] * res_own[...] + weight[1] * res_in[...]
 
 
 def body(vectors, links, directions, slice_group, peram, block_group, *, n):
@@ -323,7 +354,8 @@
     lnk = jnp.pad(links.reshape(nt, 54, sites), ((0, 0), (0, 10), (0, 0)))
     vmem = pl.BlockSpec(memory_space=pltpu.VMEM)
     smem = pl.BlockSpec(memory_space=pltpu.SMEM)
-    copies = 32
+    copies = 64
+    row_room = max(nv // n, 8)
     return pl.pallas_call(
         functools.partial(kernel, n),
         out_shape=(
@@ -344,19 +376,25 @@
             pltpu.VMEM((6 * sites, 2 * nv), bf16),
             pltpu.VMEM((6 * sites, 2 * nv), bf16),
             pltpu.VMEM((3, nv, 2 * nv), f32),
-            pltpu.VMEM((3 * nv, nv), f32),
-            pltpu.VMEM((3 * nv, nv), f32),
-            pltpu.VMEM((2, 3 * nv, nv), f32),
-            pltpu.VMEM((2, 3, 128, nv), f32),
-            pltpu.VMEM((6 * nv, 4 * cb), bf16),
-            pltpu.VMEM((6 * nv, 4 * cb), bf16),
+            pltpu.VMEM((3, nv, nv), f32),
+            pltpu.VMEM((3, nv, nv), f32),
+            pltpu.VMEM((3, nv, nv), f32),
+            pltpu.VMEM((3, 128, nv), f32),
+            pltpu.VMEM((8 * cb, 6 * nv), bf16),
+            pltpu.VMEM((8 * cb, 6 * nv), bf16),
+            pltpu.VMEM((2, cb, 4 * nv), f32),
+            pltpu.VMEM((3, 2, row_room, nv), f32),
+            pltpu.VMEM((3, 2, row_room, nv), f32),
+            pltpu.VMEM((2, cb, cb), f32),
+            pltpu.VMEM((2, cb, cb), f32),
+            pltpu.VMEM((2, cb, cb), f32),
             pltpu.SemaphoreType.DMA((copies,)),
             pltpu.SemaphoreType.DMA((copies,)),
         ],
         compiler_params=pltpu.CompilerParams(
             collective_id=0, has_side_effects=True, vmem_limit_bytes=48 * 2**20
         ),
-    )(vectors, lnk, peram, directions, slice_group, block_group)
+    )(vectors, lnk, jnp.swapaxes(peram, 1, 2), directions, slice_group, block_group)
 
 
 def solution(mesh):

time: 75 us -> 70.5 us (0.940)
  Pallas kernels: 69.7 us -> 63 us
  local copies, waits for them, and re-layouts: 3.55 us -> 5.92 us
    pallas_call x1, Pallas kernels: 69.7 us -> 63 us  [body(): pl.pallas_call(functools.partial(kernel, n), out_shape=(jax.ShapeDtypeStr...]
    unnamed x10 -> x11, local copies, waits for them, and re-layouts: 3.54 us -> 5.91 us
where the time goes in v1:
time: 70.5 us; the launch traced here: 70.2 us
  Pallas kernels  63 us (89%)
  local copies, waits for them, and re-layouts  5.92 us (8%)
  between operations  1.32 us (2%)
    pallas_call x1, Pallas kernels, body(): pl.pallas_call(functools.partial(kernel, n), out_shape=(jax.ShapeDtypeStr...  63 us
    unnamed x11, local copies, waits for them, and re-layouts  5.91 us

profile of v1, /device:TPU:0, one launch (start us, length us, event | category | flops | bytes accessed | tf_op | source)
XLA Modules:
  0.0 70.2 jit_solution(12936424651157994215)
XLA Ops:
  1.3 0.8 %copy.9 = f32[2,3,2,3,3,128]{5,0,4,3,2,1:T(2,128)S(1)} copy(f32[2,3,2,3,3,128]{5,2,4,3,1,0:T(2,128)} %param.7) | data formatting | bytes 110592 | tf_op args[1]
  2.2 0.0 copy-start
  2.2 1.4 %copy-done = f32[2,2,3,128,256]{4,3,2,1,0:T(8,128)S(1)} copy-done((f32[2,2,3,128,256]{4,3,2,1,0:T(8,128)S(1)}, f32[2,2,3,128,256]{4,3,2,1,0:T(8,128)}, u32[]{:S(2)}) %copy-start) | copy-done | bytes 1572888
  3.6 0.0 copy-start.1
  3.6 1.0 %copy-done.1 = f32[2,1024,64]{1,2,0:T(8,128)S(1)} copy-done((f32[2,1024,64]{1,2,0:T(8,128)S(1)}, f32[2,1024,64]{1,2,0:T(8,128)}, u32[]{:S(2)}) %copy-start.1) | copy-done | bytes 524312
  4.6 0.0 copy-start.2
  4.6 0.7 copy-done.2
  5.3 0.0 copy-start.3
  5.3 0.7 copy-done.3
  5.9 63.0 %shard_map.77 = (f32[2,3,2,16,256]{4,3,2,1,0:T(8,128)S(1)}, f32[2,64,64]{2,1,0:T(8,128)S(1)}) custom-call(f32[2,2,3,128,256]{4,3,2,1,0:T(8,128)S(1)} %copy-done, f32[2,64,128]{2,1,0:T(8,128)S(1)} %pad.4.lnk, f32[2,64,1024]{2,1,0:T(8,128)S(1)} %bitcast.2, s32[3]{0:T(128)S(1)} %copy-done.2, s32[2]{0:T(128)S(1)} %copy-done.3, s32[1]{0:T(128)S(6)} %copy.13.bgroup), custom_call_target="tpu_custom_call" | custom-call | tf_op jit(solution)/shard_map/pallas_call | solution.py:359
  68.9 0.7 copy.14
  69.6 0.6 copy.15
  (2 shorter events, 0.0 us)
Async XLA Ops:
  2.2 1.4 %copy-start = (f32[2,2,3,128,256]{4,3,2,1,0:T(8,128)S(1)}, f32[2,2,3,128,256]{4,3,2,1,0:T(8,128)}, u32[]{:S(2)}) copy-start(f32[2,2,3,128,256]{4,3,2,1,0:T(8,128)} %vec.1) | copy-start | bytes 4718596
  3.6 1.0 %copy-start.1 = (f32[2,1024,64]{1,2,0:T(8,128)S(1)}, f32[2,1024,64]{1,2,0:T(8,128)}, u32[]{:S(2)}) copy-start(f32[2,1024,64]{1,2,0:T(8,128)} %param.10) | copy-start | bytes 1572868
  4.6 0.7 copy-start.2
  5.3 0.7 copy-start.3

commit v2 on v1

--- a/solution.py
+++ b/solution.py
@@ -9,6 +9,7 @@
 
 NG = 2
 LZ = 16
+CHUNKS = 4
 MESH = pl.DeviceIdType.MESH
 f32 = jnp.float32
 bf16 = jnp.bfloat16
@@ -20,13 +21,14 @@
 
 
 def kernel(
-    n, vec, lnk, per, dirs, sgroup, bgroup, elem, blocks,
-    pvec, zvec, edge, plnk, zlnk, ut, lth, ltl, xh, xl, acc, part, recv, full, tcol,
+    n, vec, lnk, per_hbm, dirs, sgroup, bgroup, elem, blocks,
+    ovec, olnk, per, pvec, zvec, edge, plnk, zlnk, ut, lth, ltl, xh, xl, acc, part, recv, full, tcol,
     perh, perl, pper, rows_out, rows_in, res_own, res_out, res_in, send_sem, recv_sem,
+    vec_send, vec_recv, edge_send, edge_recv, local_sem,
 ):
     sites = vec.shape[3]
     nv = vec.shape[4]
-    cb = per.shape[1]
+    cb = per_hbm.shape[1]
     rl = nv // n
     me = lax.axis_index("space")
     cfg = lax.axis_index("cfg")
@@ -44,6 +46,12 @@
         zmasks.append(mask)
         mask *= 2
     others = [flip(1), flip(2), up, down] + [flip(m) for m in zmasks]
+    local = [
+        pltpu.make_async_copy(src, dst, local_sem.at[k])
+        for k, (src, dst) in enumerate(((vec.at[b], ovec), (lnk.at[b], olnk), (per_hbm, per)))
+    ]
+    for copy in local:
+        copy.start()
     barrier = pltpu.get_barrier_semaphore()
     for other in others:
         pl.semaphore_signal(barrier, inc=1, device_id=(cfg, other), device_id_type=MESH)
@@ -63,36 +71,54 @@
 
     partner, mate = flip(2), flip(1)
     zdst = lax.rem(me + n + 8 * b - 4, n)
-    got_edge = send(vec.at[b, :, :, pl.ds(0, LZ), :], edge.at[0], mate)
+    width = sites // CHUNKS
+
+    def piece(h):
+        return pl.ds(pl.multiple_of(h * width, width), width)
+
+    def vec_copies(h):
+        return [
+            pltpu.make_async_remote_copy(
+                src_ref=vec.at[t, :, :, piece(h), :], dst_ref=dst.at[:, :, piece(h), :],
+                send_sem=vec_send.at[k, h], recv_sem=vec_recv.at[k, h],
+                device_id=(cfg, other), device_id_type=MESH,
+            )
+            for k, (t, dst, other) in enumerate(((1 - b, pvec, partner), (b, zvec, zdst)))
+        ]
+
+    def start_vec(h):
+        for copy in vec_copies(h):
+            copy.start()
+
     got_plnk = send(lnk.at[1 - b], plnk, partner)
     got_zlnk = send(lnk.at[b], zlnk, zdst)
-    got_pvec = send(vec.at[1 - b], pvec, partner)
-    got_zvec = send(vec.at[b], zvec, zdst)
-
-    def set_left(get):
-        for ri in range(2):
-            for c in range(3):
-                j = ri * 3 + c
-                high, low = split(jnp.transpose(get(ri, c)))
-                lth[:, j * sites:(j + 1) * sites] = high
-                ltl[:, j * sites:(j + 1) * sites] = low
+    start_vec(0)
+    got_edge = send(vec.at[b, :, :, pl.ds(0, LZ), :], edge.at[0], mate)
+    start_vec(1)
+    for copy in local:
+        copy.wait()
+
+    def set_left(slot, h, source):
+        rows = [source[ri, c, piece(h), :] for ri in range(2) for c in range(3)]
+        high, low = split(jnp.transpose(jnp.concatenate(rows, axis=0)))
+        lth[slot, h] = high
+        ltl[slot, h] = low
 
     step = 16
 
-    def derive(slot, column, fetch):
-        def chunk(q, carry):
-            base = pl.multiple_of(q * step, step)
-            rows = pl.ds(base, step)
-            link = ut[slot, rows, :]
+    def derive(buf, h, slot, fetch):
+        for q in range(width // step):
+            base = pl.multiple_of(h * width + q * step, step)
+            link = ut[slot, pl.ds(base, step), :]
             out_r = [None] * 3
             out_i = [None] * 3
             for c in range(3):
-                vr = fetch(0, c, q, base)
-                vi = fetch(1, c, q, base)
+                vr = fetch(0, c, base)
+                vi = fetch(1, c, base)
                 for r in range(3):
-                    j = column + r * 3 + c
+                    j = (r * 3 + c) * 2
                     lr = jnp.broadcast_to(link[:, j:j + 1], (step, nv))
-                    li = jnp.broadcast_to(link[:, j + 9:j + 10], (step, nv))
+                    li = jnp.broadcast_to(link[:, j + 1:j + 2], (step, nv))
                     tr = lr * vr - li * vi
                     ti = lr * vi + li * vr
                     out_r[r] = tr if c == 0 else out_r[r] + tr
@@ -102,67 +128,63 @@
                 minus = out_i[r] - out_r[r]
                 ph, plo = split(plus)
                 mh, mlo = split(minus)
-                first = pl.ds(pl.multiple_of(r * sites + base, step), step)
-                second = pl.ds(pl.multiple_of((3 + r) * sites + base, step), step)
-                xh[first, :nv] = ph
-                xl[first, :nv] = plo
-                xh[second, :nv] = mh
-                xl[second, :nv] = mlo
-                xh[first, nv:] = mh
-                xl[first, nv:] = mlo
-                xh[second, nv:] = -ph
-                xl[second, nv:] = -plo
-            return carry
-
-        lax.fori_loop(0, sites // step, chunk, 0)
-
-    def contract(direction, first):
-        prod = jnp.dot(lth[...], xh[...], preferred_element_type=f32)
-        prod += jnp.dot(lth[...], xl[...], preferred_element_type=f32)
-        prod += jnp.dot(ltl[...], xh[...], preferred_element_type=f32)
-        if first:
-            acc[direction] = prod
-        else:
-            acc[direction] += prod
-
-    def set_links(slot, rows):
-        ut[slot] = jnp.transpose(rows)
-
-    def fetch_plain(get):
-        return lambda ri, c, q, base: get(ri, c, pl.ds(base, step))
-
-    def fetch_z(get):
-        def fetch(ri, c, q, base):
-            block = get(ri, c, pl.ds(base, step))
+                first = slice(r * width + q * step, r * width + (q + 1) * step)
+                second = slice((3 + r) * width + q * step, (3 + r) * width + (q + 1) * step)
+                xh[buf, first, :nv] = ph
+                xl[buf, first, :nv] = plo
+                xh[buf, second, :nv] = mh
+                xl[buf, second, :nv] = mlo
+                xh[buf, first, nv:] = mh
+                xl[buf, first, nv:] = mlo
+                xh[buf, second, nv:] = -ph
+                xl[buf, second, nv:] = -plo
+
+    def unit(buf, direction, left, h, slot, fetch):
+        derive(buf, h, slot, fetch)
+        prod = jnp.dot(lth[left, h], xh[buf], preferred_element_type=f32)
+        prod += jnp.dot(lth[left, h], xl[buf], preferred_element_type=f32)
+        prod += jnp.dot(ltl[left, h], xh[buf], preferred_element_type=f32)
+        acc[direction] += prod
+
+    def fetch_plain(source):
+        return lambda ri, c, base: source[ri, c, pl.ds(base, step), :]
+
+    def fetch_z(source):
+        def fetch(ri, c, base):
+            block = source[ri, c, pl.ds(base, step), :]
             return jnp.concatenate([block[1:], block[:1]], axis=0)
         return fetch
 
-    def fetch_y(get, k):
-        count = sites // LZ
-
-        def fetch(ri, c, q, base):
-            start = pl.multiple_of(lax.rem(q + 1, count) * step, step)
-            inner = get(ri, c, pl.ds(start, step))
-            return jnp.where(q == count - 1, edge[k, ri, c], inner)
+    def fetch_y(source, k):
+        def fetch(ri, c, base):
+            start = pl.multiple_of(lax.rem(base + step, sites), step)
+            inner = source[ri, c, pl.ds(start, step), :]
+            return jnp.where(base == sites - step, edge[k, ri, c], inner)
         return fetch
 
-    def own(ri, c, rows):
-        return vec[b, ri, c, rows, :]
-
-    def theirs(ri, c, rows):
-        return pvec[ri, c, rows, :]
-
-    def beyond(ri, c, rows):
-        return zvec[ri, c, rows, :]
-
-    everything = pl.ds(0, sites)
-    set_left(lambda ri, c: own(ri, c, everything))
-    set_links(0, lnk[b])
-    derive(0, 36, fetch_z(own))
-    contract(2, True)
+    def fetch_next(source):
+        return lambda ri, c, base: source[ri, c, pl.ds(base + step, step), :]
+
+    def rows_of_link(get):
+        return [get(r, c) for r in range(3) for c in range(3)]
+
+    def set_links(slot, pairs):
+        pairs = pairs + [jnp.zeros((64 - 18, sites), f32)]
+        ut[slot] = jnp.transpose(jnp.concatenate(pairs, axis=0))
+
+    for k in range(3):
+        acc[k] = jnp.zeros((nv, 2 * nv), f32)
+    set_links(0, rows_of_link(lambda r, c: olnk[2, r, c]))
+    set_links(1, rows_of_link(lambda r, c: olnk[1, r, c]))
     got_edge.wait()
-    derive(0, 18, fetch_y(own, 0))
-    contract(1, True)
+
+    def own_chunk(h, carry):
+        set_left(0, h, ovec)
+        unit(0, 2, 0, h, 0, fetch_z(ovec))
+        unit(1, 1, 0, h, 1, fetch_y(ovec, 0))
+        return carry
+
+    lax.fori_loop(0, CHUNKS, own_chunk, 0)
 
     def set_peram(slot, source):
         lo = [[source[ri, :, (2 + s) * nv:(3 + s) * nv] for ri in range(2)] for s in range(2)]
@@ -184,21 +206,17 @@
 
     got_plnk.wait()
     got_zlnk.wait()
-    set_links(1, plnk[...])
+    set_links(2, rows_of_link(lambda r, c: plnk[2, r, c]))
+    set_links(3, rows_of_link(lambda r, c: plnk[1, r, c]))
+    sign = jnp.where(lax.broadcasted_iota(jnp.int32, (2, sites), 0) == 0, -1.0, 1.0)
 
     def turn(ahead, behind):
-        rows = []
-        for ri in range(2):
-            for r in range(3):
-                for c in range(3):
-                    j, k = ri * 9 + r * 3 + c, ri * 9 + c * 3 + r
-                    back = -behind[k:k + 1] if ri == 0 else behind[k:k + 1]
-                    rows.append(jnp.where(b == 0, ahead[j:j + 1], back))
-        rows.append(jnp.zeros((64 - 18, sites), f32))
-        return jnp.concatenate(rows, axis=0)
-
-    set_links(2, turn(lnk[b, 0:18], plnk[0:18]))
-    set_links(3, turn(plnk[0:18], zlnk[0:18]))
+        return rows_of_link(
+            lambda r, c: jnp.where(b == 0, ahead[0, r, c], sign * behind[0, c, r])
+        )
+
+    set_links(4, turn(olnk, plnk))
+    set_links(5, turn(plnk, zlnk))
 
     stages = [1] + zmasks
 
@@ -233,29 +251,51 @@
     def finish(k):
         part[k] = acc[k, :, :nv] + jnp.transpose(acc[k, :, nv:])
 
-    got_pvec.wait()
-    got_pedge = send(pvec.at[:, :, pl.ds(0, LZ), :], edge.at[1], mate)
+    def edge_copy():
+        return pltpu.make_async_remote_copy(
+            src_ref=pvec.at[:, :, pl.ds(0, LZ), :], dst_ref=edge.at[1],
+            send_sem=edge_send, recv_sem=edge_recv,
+            device_id=(cfg, mate), device_id_type=MESH,
+        )
+
+    def chunk_x(h):
+        unit(0, 0, 0, h, 4, fetch_plain(pvec))
+        unit(1, 0, 1, h, 5, fetch_plain(zvec))
+
+    def chunk_z(h):
+        set_left(1, h, pvec)
+        unit(0, 2, 1, h, 2, fetch_z(pvec))
+
+    def arrived(h):
+        for copy in vec_copies(h):
+            copy.wait()
+
+    def their_chunk(h, carry):
+        arrived(h)
+        if CHUNKS > 2:
+            pl.when(h + 2 < CHUNKS)(lambda: start_vec(h + 2))
+        pl.when(h == 0)(lambda: edge_copy().start())
+        chunk_z(h)
+        chunk_x(h)
+        pl.when(h > 0)(lambda: unit(0, 1, 1, h - 1, 3, fetch_next(pvec)))
+        return carry
+
+    last = CHUNKS - 1
+    lax.fori_loop(0, last, their_chunk, 0)
+    arrived(last)
     got_pper = send(per, pper, partner)
-    derive(2, 0, fetch_plain(theirs))
-    contract(0, True)
-    set_left(lambda ri, c: theirs(ri, c, everything))
-    derive(1, 36, fetch_z(theirs))
-    contract(2, False)
+    chunk_z(last)
     finish(2)
     moving_z = reduce_and_share(2)
     next(moving_z)
-    got_pedge.wait()
-    derive(1, 18, fetch_y(theirs, 1))
+    edge_copy().wait()
+    unit(1, 1, 1, last - 1, 3, fetch_next(pvec))
+    unit(0, 1, 1, last, 3, fetch_y(pvec, 1))
+    finish(1)
     next(moving_z)
-    contract(1, False)
-    finish(1)
     moving_y = reduce_and_share(1)
     next(moving_y)
-    got_zvec.wait()
-    derive(3, 0, fetch_plain(beyond))
-    next(moving_z)
-    next(moving_y)
-    contract(0, False)
+    chunk_x(last)
     finish(0)
     moving_x = reduce_and_share(0)
     moving = [moving_z, moving_y, moving_x]
@@ -351,7 +391,8 @@
 def body(vectors, links, directions, slice_group, peram, block_group, *, n):
     nt, _, _, sites, nv = vectors.shape
     cb = peram.shape[2]
-    lnk = jnp.pad(links.reshape(nt, 54, sites), ((0, 0), (0, 10), (0, 0)))
+    lnk = jnp.transpose(links, (0, 1, 3, 4, 2, 5))
+    hbm = pl.BlockSpec(memory_space=pltpu.HBM)
     vmem = pl.BlockSpec(memory_space=pltpu.VMEM)
     smem = pl.BlockSpec(memory_space=pltpu.SMEM)
     copies = 64
@@ -362,19 +403,22 @@
             jax.ShapeDtypeStruct((NG, 3, 2, nv // n, nv), f32),
             jax.ShapeDtypeStruct((2, cb, cb), f32),
         ),
-        in_specs=[vmem, vmem, vmem, smem, smem, smem],
+        in_specs=[hbm, hbm, hbm, smem, smem, smem],
         out_specs=(vmem, vmem),
         scratch_shapes=[
             pltpu.VMEM((2, 3, sites, nv), f32),
+            pltpu.VMEM((3, 3, 3, 2, sites), f32),
+            pltpu.VMEM((2, cb, 4 * nv), f32),
+            pltpu.VMEM((2, 3, sites, nv), f32),
             pltpu.VMEM((2, 3, sites, nv), f32),
             pltpu.VMEM((2, 2, 3, LZ, nv), f32),
-            pltpu.VMEM((64, sites), f32),
-            pltpu.VMEM((64, sites), f32),
-            pltpu.VMEM((4, sites, 64), f32),
-            pltpu.VMEM((nv, 6 * sites), bf16),
-            pltpu.VMEM((nv, 6 * sites), bf16),
-            pltpu.VMEM((6 * sites, 2 * nv), bf16),
-            pltpu.VMEM((6 * sites, 2 * nv), bf16),
+            pltpu.VMEM((3, 3, 3, 2, sites), f32),
+            pltpu.VMEM((3, 3, 3, 2, sites), f32),
+            pltpu.VMEM((6, sites, 64), f32),
+            pltpu.VMEM((2, CHUNKS, nv, 6 * sites // CHUNKS), bf16),
+            pltpu.VMEM((2, CHUNKS, nv, 6 * sites // CHUNKS), bf16),
+            pltpu.VMEM((2, 6 * sites // CHUNKS, 2 * nv), bf16),
+            pltpu.VMEM((2, 6 * sites // CHUNKS, 2 * nv), bf16),
             pltpu.VMEM((3, nv, 2 * nv), f32),
             pltpu.VMEM((3, nv, nv), f32),
             pltpu.VMEM((3, nv, nv), f32),
@@ -390,6 +434,11 @@
             pltpu.VMEM((2, cb, cb), f32),
             pltpu.SemaphoreType.DMA((copies,)),
             pltpu.SemaphoreType.DMA((copies,)),
+            pltpu.SemaphoreType.DMA((2, CHUNKS)),
+            pltpu.SemaphoreType.DMA((2, CHUNKS)),
+            pltpu.SemaphoreType.DMA,
+            pltpu.SemaphoreType.DMA,
+            pltpu.SemaphoreType.DMA((3,)),
         ],
         compiler_params=pltpu.CompilerParams(
             collective_id=0, has_side_effects=True, vmem_limit_bytes=48 * 2**20

time: 70.5 us -> 69.6 us (0.987)
  Pallas kernels: 63 us -> 62.1 us
    pallas_call x1, Pallas kernels: 63 us -> 62.1 us  [body(): pl.pallas_call(functools.partial(kernel, n), out_shape=(jax.ShapeDtypeStr...]
    unnamed x11 -> x12, local copies, waits for them, and re-layouts: 5.91 us -> 5.87 us
where the time goes in v2:
time: 69.6 us; the launch traced here: 69.3 us
  Pallas kernels  62.1 us (89%)
  local copies, waits for them, and re-layouts  5.87 us (8%)
  between operations  1.3 us (2%)
    pallas_call x1, Pallas kernels, body(): pl.pallas_call(functools.partial(kernel, n), out_shape=(jax.ShapeDtypeStr...  62.1 us
    unnamed x12, local copies, waits for them, and re-layouts  5.87 us

profile of v2, /device:TPU:0, one launch (start us, length us, event | category | flops | bytes accessed | tf_op | source)
XLA Modules:
  0.0 69.3 jit_solution(996407152025472437)
XLA Ops:
  1.3 0.0 copy-start
  1.3 1.4 %copy-done = f32[2,2,3,128,256]{4,3,2,1,0:T(8,128)S(1)} copy-done((f32[2,2,3,128,256]{4,3,2,1,0:T(8,128)S(1)}, f32[2,2,3,128,256]{4,3,2,1,0:T(8,128)}, u32[]{:S(2)}) %copy-start) | copy-done | bytes 1572888
  2.7 0.0 copy-start.1
  2.7 1.0 %copy-done.1 = f32[2,1024,64]{1,2,0:T(8,128)S(1)} copy-done((f32[2,1024,64]{1,2,0:T(8,128)S(1)}, f32[2,1024,64]{1,2,0:T(8,128)}, u32[]{:S(2)}) %copy-start.1) | copy-done | bytes 524312
  3.7 0.0 copy-start.2
  3.7 0.8 %copy-done.2 = f32[2,3,2,3,3,128]{5,2,4,3,1,0:T(2,128)S(1)} copy-done((f32[2,3,2,3,3,128]{5,2,4,3,1,0:T(2,128)S(1)}, f32[2,3,2,3,3,128]{5,2,4,3,1,0:T(2,128)}, u32[]{:S(2)}) %copy-start.2) | copy-done | bytes 55320
  4.5 0.0 copy-start.3
  4.5 0.7 copy-done.3
  5.2 0.0 copy-start.4
  5.2 0.7 copy-done.4
  5.9 62.1 %shard_map.77 = (f32[2,3,2,16,256]{4,3,2,1,0:T(8,128)S(1)}, f32[2,64,64]{2,1,0:T(8,128)S(1)}) custom-call(f32[2,2,3,128,256]{4,3,2,1,0:T(8,128)S(1)} %copy-done, f32[2,3,3,3,2,128]{5,4,3,2,1,0:T(2,128)S(1)} %bitcast.3, f32[2,64,1024]{2,1,0:T(8,128)S(1)} %bitcast.2, s32[3]{0:T(128)S(1)} %copy-done.3, s32[2]{0:T(128)S(1)} %copy-done.4, s32[1]{0:T(128)S(6)} %copy.10.bgroup), custom_call_target="tpu_custom_call" | custom-call | tf_op jit(solution)/shard_map/pallas_call | solution.py:400
  68.0 0.7 copy.11
  68.7 0.6 copy.12
Async XLA Ops:
  1.3 1.4 %copy-start = (f32[2,2,3,128,256]{4,3,2,1,0:T(8,128)S(1)}, f32[2,2,3,128,256]{4,3,2,1,0:T(8,128)}, u32[]{:S(2)}) copy-start(f32[2,2,3,128,256]{4,3,2,1,0:T(8,128)} %vec.1) | copy-start | bytes 4718596
  2.7 1.0 %copy-start.1 = (f32[2,1024,64]{1,2,0:T(8,128)S(1)}, f32[2,1024,64]{1,2,0:T(8,128)}, u32[]{:S(2)}) copy-start(f32[2,1024,64]{1,2,0:T(8,128)} %param.10) | copy-start | bytes 1572868
  3.7 0.8 %copy-start.2 = (f32[2,3,2,3,3,128]{5,2,4,3,1,0:T(2,128)S(1)}, f32[2,3,2,3,3,128]{5,2,4,3,1,0:T(2,128)}, u32[]{:S(2)}) copy-start(f32[2,3,2,3,3,128]{5,2,4,3,1,0:T(2,128)} %param.7) | copy-start | bytes 165892
  4.5 0.7 copy-start.3
  5.2 0.7 copy-start.4

commit v3 on v2

--- a/solution.py
+++ b/solution.py
@@ -441,7 +441,7 @@
             pltpu.SemaphoreType.DMA((3,)),
         ],
         compiler_params=pltpu.CompilerParams(
-            collective_id=0, has_side_effects=True, vmem_limit_bytes=48 * 2**20
+            collective_id=0, has_side_effects=True, vmem_limit_bytes=63 * 2**20
         ),
     )(vectors, lnk, jnp.swapaxes(peram, 1, 2), directions, slice_group, block_group)
 

time: 69.6 us -> 67.6 us (0.971)
  local copies, waits for them, and re-layouts: 5.87 us -> 3.09 us
  Pallas kernels: 62.1 us -> 63 us
    unnamed x12 -> x2, local copies, waits for them, and re-layouts: 5.87 us -> 3.09 us
    pallas_call x1, Pallas kernels: 62.1 us -> 63 us  [body(): pl.pallas_call(functools.partial(kernel, n), out_shape=(jax.ShapeDtypeStr...]
where the time goes in v3:
time: 67.6 us; the launch traced here: 67.4 us
  Pallas kernels  63 us (93%)
  local copies, waits for them, and re-layouts  3.09 us (5%)
  between operations  1.29 us (2%)
    pallas_call x1, Pallas kernels, body(): pl.pallas_call(functools.partial(kernel, n), out_shape=(jax.ShapeDtypeStr...  63 us
    unnamed x2, local copies, waits for them, and re-layouts  3.09 us

profile of v3, /device:TPU:0, one launch (start us, length us, event | category | flops | bytes accessed | tf_op | source)
XLA Modules:
  0.0 67.4 jit_solution(17589569930573301718)
XLA Ops:
  1.3 63.0 %shard_map.77 = (f32[2,3,2,16,256]{4,3,2,1,0:T(8,128)}, f32[2,64,64]{2,1,0:T(8,128)}) custom-call(f32[2,2,3,128,256]{4,3,2,1,0:T(8,128)} %vec.1, f32[2,3,3,3,2,128]{5,4,3,2,1,0:T(2,128)} %bitcast.3, f32[2,64,1024]{2,1,0:T(8,128)} %bitcast.2, s32[3]{0:T(128)} %dirs.1, s32[2]{0:T(128)} %sgroup.1, s32[1]{0:T(128)S(6)} %copy.10.bgroup), custom_call_target="tpu_custom_call" | custom-call | tf_op jit(solution)/shard_map/pallas_call | solution.py:400
  64.3 1.6 %copy.11 = f32[2,3,2,16,256]{4,3,2,1,0:T(8,128)} copy(f32[2,3,2,16,256]{4,3,2,1,0:T(8,128)} %get-tuple-element.4) | data formatting | bytes 393216
  65.9 1.5 %copy.12 = f32[2,64,64]{2,1,0:T(8,128)} copy(f32[2,64,64]{2,1,0:T(8,128)} %get-tuple-element.5) | data formatting | bytes 65536
